TPU v7x, 512 devices: a whole 4x8x8 slice. The times are simulated.
512 devices in a mesh: dom: 128 (over y, z, core), row: 4 (over x).
Axes of the slice: x: 4, y: 8, z: 8, core: 2. Of those that a mesh axis runs over, the one named last changes fastest.
Arguments:
- p_blocks: bfloat16 [1536, 12, 128, 128], P(('dom', 'row')), may hold values from -0.5 to 0.5
- p_cols: int32 [1536, 12], P(('dom', 'row')), may hold values from 0 to 1535, as said below
- sel_square: int32 [1536, 4, 12], P(('dom', 'row')), may hold values from -1 to 1, as said below
- sel_cube: int32 [1536, 4, 12], P(('dom', 'row')), may hold values from -1 to 3, as said below
Outputs:
- purified: bfloat16 [1536, 4, 128, 128], P(('dom', 'row'))
Inputs may be any that keep to these rules, and one draw needn't show every extreme that they name: `p_cols`: the 12 entries of a row are distinct clusters held by devices at most 2 positions away from the row's own device in dom-then-row order, cyclically. `sel_square`: -1 marks a term left out; other values name one of the first 2 stored blocks of row p_cols[i, a]. `sel_cube`: -1 marks a term left out; other values name a block of square of row p_cols[i, a].
All inputs are finite; a program needn't handle non-finite values.
Results may differ from a plain program's by a relative error of at most 0.0043.
Values may be sent and summed in bfloat16 or wider, within the bound.
A program may use at most 64 MiB of HBM per device.

v0:
```python
import functools

import jax
import jax.numpy as jnp
from jax import lax
from jax.experimental import pallas as pl
from jax.experimental.pallas import tpu as pltpu
from jax.sharding import PartitionSpec as P

MW = 2
REACH = 2
NEAR = 2 * REACH + 1
SLOTS = NEAR + 1
RIGHT, LEFT, OPPOSITE, ACROSS, SIDE = range(5)


class Spread:
    def __init__(self, buffer, chunks, sems, place):
        self.buffer, self.chunks = buffer, chunks
        self.send_sem, self.recv_sem = sems
        self.x, self.right, self.left, self.across, self.spot = place

    def copy(self, way, k):
        x = self.x
        cut, passed = self.chunks[k]
        opposite = 4 - 4 * (x // 2)
        if way == RIGHT:
            there = lax.rem(x + 1, 4)
            source, target, device = 2, 5 - 4 * ((there + 3) // 4), {"row": self.right}
        elif way == LEFT:
            there = lax.rem(x + 3, 4)
            source, target, device = 2, 3 + 2 * (there // 3), {"row": self.left}
        elif way == OPPOSITE:
            if passed == RIGHT:
                there = lax.rem(x + 1, 4)
                source, device = 5 - 4 * ((x + 3) // 4), {"row": self.right}
            else:
                there = lax.rem(x + 3, 4)
                source, device = 3 + 2 * (x // 3), {"row": self.left}
            target = 4 - 4 * (there // 2)
        elif way == ACROSS:
            source, target, device = opposite, 4 - opposite, {"dom": self.across}
        else:
            source, target, device = 5, 1 + 2 * (x // 3), {"dom": self.across}
        return pltpu.make_async_remote_copy(
            src_ref=cut(self.buffer, source),
            dst_ref=cut(self.buffer, target),
            send_sem=self.send_sem.at[way, k],
            recv_sem=self.recv_sem.at[way, k],
            device_id=device,
            device_id_type=pl.DeviceIdType.MESH,
        )

    def at_end(self, end, way, k, action):
        @pl.when(self.x == end)
        def _():
            getattr(self.copy(way, k), action)()

    def part(self, part):
        return range(len(self.chunks)) if part is None else part

    def send_passed(self, part=None):
        for k in self.part(part):
            self.copy(self.chunks[k][1], k).start()

    def send_urgent(self, part=None):
        for spot, way in ((0, LEFT), (7, RIGHT)):
            @pl.when(self.spot == spot)
            def _():
                for k in self.part(part):
                    if self.chunks[k][1] != way:
                        self.copy(way, k).start()

    def send_rest(self, part=None):
        for spot, way in ((0, LEFT), (7, RIGHT)):
            @pl.when(self.spot != spot)
            def _():
                for k in self.part(part):
                    if self.chunks[k][1] != way:
                        self.copy(way, k).start()

    def pass_on(self, part=None, sides=True):
        for k in self.part(part):
            self.copy(self.chunks[k][1], k).wait_recv()
            self.copy(OPPOSITE, k).start()
            if sides:
                self.send_sides((k,))

    def send_sides(self, part=None):
        for k in self.part(part):
            self.at_end(0 if self.chunks[k][1] == RIGHT else 3, SIDE, k, "start")

    def take_rest(self, part=None):
        for k in self.part(part):
            way = LEFT + RIGHT - self.chunks[k][1]
            self.copy(way, k).wait_recv()
            self.at_end(0 if way == RIGHT else 3, SIDE, k, "start")

    def send_across(self, part=None):
        for k in self.part(part):
            self.copy(OPPOSITE, k).wait_recv()
            self.copy(ACROSS, k).start()

    def take_across(self, part=None):
        for k in self.part(part):
            self.at_end(0, SIDE, k, "wait_recv")
            self.at_end(3, SIDE, k, "wait_recv")
            self.copy(ACROSS, k).wait_recv()

    def finish(self):
        for k in range(len(self.chunks)):
            for way in (RIGHT, LEFT, OPPOSITE, ACROSS):
                self.copy(way, k).wait_send()
            self.at_end(0, SIDE, k, "wait_send")
            self.at_end(3, SIDE, k, "wait_send")


def swapped(tile):
    half = tile.shape[1] // 2
    return jnp.concatenate([tile[:, half:], tile[:, :half]], axis=1)


def joined(first, second):
    half = first.shape[1] // 2
    return jnp.concatenate([first[:, :half], second[:, half:]], axis=1)


def place_picks(places, cols_ref, sel_ref, tiles, zero, origin, clusters, reach_rows):
    rows, products, count = sel_ref.shape
    turned = zero + 1

    def one(a, carry):
        for i in range(rows):
            near = cols_ref[i, a] - origin
            near = jnp.where(near < 0, near + clusters, near)
            near = jnp.where(near >= clusters, near - clusters, near)
            base = jnp.minimum(near, reach_rows - 1) * tiles
            for s in range(products):
                picked = sel_ref[i, s, a]
                odd = lax.bitwise_and(picked, 1)
                turn = odd if s % 2 == 0 else 1 - odd
                tile = base + lax.shift_right_arithmetic(picked, 1) + turned * turn
                places[(i * count + a) * products + s] = jnp.where(picked >= 0, tile, zero)
        return carry

    lax.fori_loop(0, count, one, 0)


def contract(blocks, nearby, places, row, products):
    count = blocks.shape[1]
    total = None
    for pair in range(0, count, 2):
        left = jnp.concatenate([blocks[row, pair], blocks[row, pair + 1]], axis=1)
        right = []
        for a in (pair, pair + 1):
            at = (row * count + a) * products
            line = [joined(nearby[places[at + s]], nearby[places[at + s + 1]]) for s in range(0, products, 2)]
            right.append(jnp.concatenate(line, axis=1))
        term = jnp.dot(left, jnp.concatenate(right, axis=0), preferred_element_type=jnp.float32)
        total = term if total is None else total + term
    return total


def kernel(
    doms, p_hbm, cols_hbm, sel_square_hbm, sel_cube_hbm, out_ref,
    blocks, cols_ref, sel_square_ref, sel_cube_ref, window_places, square_places, window0, window1, square0, square1, total, first_out,
    local_sem, go_sem, window_send, window_recv, square_send, square_recv,
):
    rows, products, size = out_ref.shape[:3]
    half = size // 2
    x, dom = lax.axis_index("row"), lax.axis_index("dom")
    ahead, behind = lax.rem(dom + 1, doms), lax.rem(dom + doms - 1, doms)
    right, left = lax.rem(x + 1, 4), lax.rem(x + 3, 4)
    across = lax.rem(dom + doms + 1 - 2 * (x // 2), doms)
    clusters = doms * 4 * rows
    origin = ((dom * 4 + x) - REACH) * rows
    reach_rows = NEAR * rows

    own = pltpu.make_async_copy(p_hbm.at[:, pl.ds(0, MW)], blocks.at[:, pl.ds(0, MW)], local_sem.at[0])
    rest = blocks.shape[1] - MW
    others = [
        pltpu.make_async_copy(p_hbm.at[:, pl.ds(MW, rest)], blocks.at[:, pl.ds(MW, rest)], local_sem.at[1]),
        pltpu.make_async_copy(cols_hbm, cols_ref, local_sem.at[2]),
        pltpu.make_async_copy(sel_square_hbm, sel_square_ref, local_sem.at[3]),
        pltpu.make_async_copy(sel_cube_hbm, sel_cube_ref, local_sem.at[4]),
    ]
    own.start()
    for load in others:
        load.start()

    barrier = pltpu.get_barrier_semaphore()
    for device in ({"row": right}, {"row": left}, {"dom": behind}):
        pl.semaphore_signal(barrier, inc=1, device_id=device, device_id_type=pl.DeviceIdType.MESH)

    tiles = products // 2
    zero_w, zero_q = SLOTS * rows, SLOTS * rows * tiles
    windows, squares = (window0, window1), (square0, square1)
    for buffer, zero in ((window0, zero_w), (window1, zero_w), (square0, zero_q), (square1, zero_q)):
        buffer[zero] = jnp.zeros((size, size), buffer.dtype)
    own.wait()
    for i in range(rows):
        one, two = blocks[i, 0], blocks[i, 1]
        window0[REACH * rows + i] = joined(one, swapped(two))
        window1[REACH * rows + i] = joined(swapped(one), two)

    place = (x, right, left, across, x + 4 * lax.rem(dom, 2))

    def window_cut(tile, part):
        return lambda buffer, slot: buffer.at[slot * rows + tile, pl.ds(part * half, half)]

    def square_cut(tile):
        return lambda buffer, slot: buffer.at[slot * rows * tiles + tile]

    window_chunks = [(window_cut(tile, part), (RIGHT, LEFT)[part]) for tile in range(rows) for part in (0, 1)]
    square_chunks = [(square_cut(tile), RIGHT if tile % 2 == 0 else LEFT) for tile in range(rows * tiles)]
    w0, w1 = (Spread(windows[h], window_chunks, (window_send.at[h], window_recv.at[h]), place) for h in (0, 1))
    q0, q1 = (Spread(squares[h], square_chunks, (square_send.at[h], square_recv.at[h]), place) for h in (0, 1))

    def turn(buffer, tiles, zero):
        for tile in range(reach_rows * tiles):
            buffer[zero + 1 + tile] = swapped(buffer[tile])

    def make_square(h, spread):
        turn(windows[h], 1, zero_w)
        for i in range(rows):
            value = contract(blocks, windows[h], window_places, i, products)
            total[h, i] = value
            for t in range(tiles):
                squares[h][(REACH * rows + i) * tiles + t] = value[:, t * size:(t + 1) * size].astype(jnp.bfloat16)
            part = range(i * tiles, (i + 1) * tiles)
            spread.send_passed(part)
        spread.send_urgent()

    def purified(h, i):
        value = contract(blocks, squares[h], square_places, i, products)
        return (3.0 * total[h, i] - 2.0 * value).astype(out_ref.dtype)

    pl.semaphore_wait(barrier, 3)

    @pl.when(x >= 2)
    def _():
        pl.semaphore_signal(go_sem, inc=1, device_id={"dom": ahead}, device_id_type=pl.DeviceIdType.MESH)

    w0.send_passed()
    w0.send_urgent()
    w0.send_rest((0, 1))
    w0.pass_on((0, 1), False)
    w0.send_rest((2, 3))
    w0.pass_on((2, 3), False)
    w0.send_rest((4, 5))
    w0.pass_on((4, 5), False)
    w1.send_passed()
    w1.send_urgent()
    for load in others:
        load.wait()
    place_picks(window_places, cols_ref, sel_square_ref, 1, zero_w, origin, clusters, reach_rows)

    @pl.when(x >= 2)
    def _():
        pl.semaphore_wait(go_sem, 1)

    w0.send_sides()
    w0.take_rest()
    w0.send_across()
    w1.pass_on()
    w1.send_rest()
    place_picks(square_places, cols_ref, sel_cube_ref, tiles, zero_q, origin, clusters, reach_rows)
    w0.take_across()
    make_square(0, q0)
    w1.take_rest()
    w1.send_across()
    q0.pass_on()
    q0.send_rest()
    w1.take_across()
    make_square(1, q1)
    q0.take_rest()
    q0.send_across()
    q1.pass_on()
    q1.send_rest()
    q0.take_across()
    turn(square0, tiles, zero_q)
    for i in range(rows):
        first_out[i] = purified(0, i)
    q1.send_across()
    q1.take_rest()
    q1.take_across()
    turn(square1, tiles, zero_q)
    for i in range(rows):
        early, late = first_out[i], purified(1, i)
        for t in range(tiles):
            one, two = early[:, t * size:(t + 1) * size], late[:, t * size:(t + 1) * size]
            out_ref[i, 2 * t] = joined(one, swapped(two))
            out_ref[i, 2 * t + 1] = joined(swapped(one), two)
    for spread in (w0, w1, q0, q1):
        spread.finish()


def solution(mesh):
    doms, row_devices = mesh.shape["dom"], mesh.shape["row"]
    assert row_devices == 4

    def per_device(p_blocks, p_cols, sel_square, sel_cube):
        rows, count, size, _ = p_blocks.shape
        products = sel_square.shape[1]
        tiles = products // 2
        flops = 2 * 2 * rows * products * count * size**3
        window_tiles = (SLOTS + NEAR) * rows + 1
        square_tiles = (SLOTS + NEAR) * rows * tiles + 1
        return pl.pallas_call(
            functools.partial(kernel, doms),
            out_shape=jax.ShapeDtypeStruct((rows, products, size, size), jnp.bfloat16),
            in_specs=[pl.BlockSpec(memory_space=pltpu.HBM)] * 4,
            out_specs=pl.BlockSpec(memory_space=pltpu.VMEM),
            scratch_shapes=[
                pltpu.VMEM((rows, count, size, size), jnp.bfloat16),
                pltpu.SMEM(p_cols.shape, jnp.int32),
                pltpu.SMEM(sel_square.shape, jnp.int32),
                pltpu.SMEM(sel_cube.shape, jnp.int32),
                pltpu.SMEM((rows * count * products,), jnp.int32),
                pltpu.SMEM((rows * count * products,), jnp.int32),
                pltpu.VMEM((window_tiles, size, size), jnp.bfloat16),
                pltpu.VMEM((window_tiles, size, size), jnp.bfloat16),
                pltpu.VMEM((square_tiles, size, size), jnp.bfloat16),
                pltpu.VMEM((square_tiles, size, size), jnp.bfloat16),
                pltpu.VMEM((2, rows, size, tiles * size), jnp.float32),
                pltpu.VMEM((rows, size, tiles * size), jnp.bfloat16),
                pltpu.SemaphoreType.DMA((5,)),
                pltpu.SemaphoreType.REGULAR,
                pltpu.SemaphoreType.DMA((2, 5, 2 * rows)),
                pltpu.SemaphoreType.DMA((2, 5, 2 * rows)),
                pltpu.SemaphoreType.DMA((2, 5, rows * tiles)),
                pltpu.SemaphoreType.DMA((2, 5, rows * tiles)),
            ],
            cost_estimate=pl.CostEstimate(flops=flops, bytes_accessed=4 * p_blocks.size, transcendentals=0),
            compiler_params=pltpu.CompilerParams(
                collective_id=0, has_side_effects=True, vmem_limit_bytes=60 * 1024 * 1024
            ),
        )(p_blocks, p_cols, sel_square, sel_cube)

    return jax.shard_map(
        per_device,
        mesh=mesh,
        in_specs=(
            P(("dom", "row"), None, None, None),
            P(("dom", "row"), None),
            P(("dom", "row"), None, None),
            P(("dom", "row"), None, None),
        ),
        out_specs=P(("dom", "row"), None, None, None),
        check_vma=False,
    )
```

profile of v0, /device:TPU:1, one launch (start us, length us, event | category | flops | bytes accessed | tf_op | source)
XLA Modules:
  0.0 45.7 jit_solution(2705902862593869176)
XLA Ops:
  0.0 43.9 %shard_map.46 = bf16[3,4,128,128]{3,2,1,0:T(8,128)(2,1)} custom-call(bf16[3,12,128,128]{3,2,1,0:T(8,128)(2,1)} %p_hbm.1, s32[3,12]{1,0:T(4,128)} %cols_hbm.1, s32[3,4,12]{2,1,0:T(4,128)} %sel_square_hbm.1, s32[3,4,12]{2,1,0:T(4,128)} %sel_cube_hbm.1), custom_call_target="tpu_custom_call" | custom-call | flops 1207959552 | bytes 2359296 | tf_op jit(solution)/shard_map/pallas_call | solution.py:309
  43.9 1.8 %copy.6 = bf16[3,4,128,128]{3,2,1,0:T(8,128)(2,1)} copy(bf16[3,4,128,128]{3,2,1,0:T(8,128)(2,1)} %shard_map.46) | data formatting | bytes 786432
where the time goes:
time: 45.9 us; the launch traced here: 45.7 us
  Pallas kernels  43.9 us (96%)
  local copies, waits for them, and re-layouts  1.77 us (4%)
    pallas_call x1, Pallas kernels, per_device(): pl.pallas_call(functools.partial(kernel, doms), out_shape=jax.ShapeDtypeS...  43.9 us
    unnamed x1, local copies, waits for them, and re-layouts  1.77 us

commit v1 on v0

--- a/solution.py
+++ b/solution.py
@@ -162,9 +162,9 @@
 
 
 def kernel(
-    doms, p_hbm, cols_hbm, sel_square_hbm, sel_cube_hbm, out_ref,
-    blocks, cols_ref, sel_square_ref, sel_cube_ref, window_places, square_places, window0, window1, square0, square1, total, first_out,
-    local_sem, go_sem, window_send, window_recv, square_send, square_recv,
+    doms, p_hbm, cols_hbm, sel_square_hbm, sel_cube_hbm, out_hbm,
+    blocks, cols_ref, sel_square_ref, sel_cube_ref, window_places, square_places, window0, window1, square0, square1, total, first_out, out_ref,
+    local_sem, out_sem, go_sem, window_send, window_recv, square_send, square_recv,
 ):
     rows, products, size = out_ref.shape[:3]
     half = size // 2
@@ -216,12 +216,16 @@
     w0, w1 = (Spread(windows[h], window_chunks, (window_send.at[h], window_recv.at[h]), place) for h in (0, 1))
     q0, q1 = (Spread(squares[h], square_chunks, (square_send.at[h], square_recv.at[h]), place) for h in (0, 1))
 
-    def turn(buffer, tiles, zero):
-        for tile in range(reach_rows * tiles):
-            buffer[zero + 1 + tile] = swapped(buffer[tile])
+    def turn(buffer, unit, zero, slots):
+        for slot in slots:
+            for tile in range(unit):
+                buffer[zero + 1 + slot * unit + tile] = swapped(buffer[slot * unit + tile])
+
+    sooner = (2, 5 - 4 * ((x + 3) // 4), 3 + 2 * (x // 3), 4 - 4 * (x // 2))
+    later = (4 * (x // 2), 1 + 2 * (x // 3))
 
     def make_square(h, spread):
-        turn(windows[h], 1, zero_w)
+        turn(windows[h], rows, zero_w, later)
         for i in range(rows):
             value = contract(blocks, windows[h], window_places, i, products)
             total[h, i] = value
@@ -265,34 +269,40 @@
     w1.pass_on()
     w1.send_rest()
     place_picks(square_places, cols_ref, sel_cube_ref, tiles, zero_q, origin, clusters, reach_rows)
+    turn(window0, rows, zero_w, sooner)
     w0.take_across()
     make_square(0, q0)
     w1.take_rest()
     w1.send_across()
     q0.pass_on()
     q0.send_rest()
+    turn(window1, rows, zero_w, sooner)
     w1.take_across()
     make_square(1, q1)
+    q0.send_across()
     q0.take_rest()
-    q0.send_across()
     q1.pass_on()
     q1.send_rest()
     q0.take_across()
-    turn(square0, tiles, zero_q)
+    turn(square0, rows * tiles, zero_q, sooner + later)
     for i in range(rows):
         first_out[i] = purified(0, i)
     q1.send_across()
     q1.take_rest()
+    turn(square1, rows * tiles, zero_q, sooner)
     q1.take_across()
-    turn(square1, tiles, zero_q)
+    turn(square1, rows * tiles, zero_q, later)
     for i in range(rows):
         early, late = first_out[i], purified(1, i)
         for t in range(tiles):
             one, two = early[:, t * size:(t + 1) * size], late[:, t * size:(t + 1) * size]
             out_ref[i, 2 * t] = joined(one, swapped(two))
             out_ref[i, 2 * t + 1] = joined(swapped(one), two)
+        pltpu.make_async_copy(out_ref.at[i], out_hbm.at[i], out_sem.at[i]).start()
     for spread in (w0, w1, q0, q1):
         spread.finish()
+    for i in range(rows):
+        pltpu.make_async_copy(out_ref.at[i], out_hbm.at[i], out_sem.at[i]).wait()
 
 
 def solution(mesh):
@@ -304,13 +314,13 @@
         products = sel_square.shape[1]
         tiles = products // 2
         flops = 2 * 2 * rows * products * count * size**3
-        window_tiles = (SLOTS + NEAR) * rows + 1
-        square_tiles = (SLOTS + NEAR) * rows * tiles + 1
+        window_tiles = 2 * SLOTS * rows + 1
+        square_tiles = 2 * SLOTS * rows * tiles + 1
         return pl.pallas_call(
             functools.partial(kernel, doms),
             out_shape=jax.ShapeDtypeStruct((rows, products, size, size), jnp.bfloat16),
             in_specs=[pl.BlockSpec(memory_space=pltpu.HBM)] * 4,
-            out_specs=pl.BlockSpec(memory_space=pltpu.VMEM),
+            out_specs=pl.BlockSpec(memory_space=pl.ANY),
             scratch_shapes=[
                 pltpu.VMEM((rows, count, size, size), jnp.bfloat16),
                 pltpu.SMEM(p_cols.shape, jnp.int32),
@@ -324,7 +334,9 @@
                 pltpu.VMEM((square_tiles, size, size), jnp.bfloat16),
                 pltpu.VMEM((2, rows, size, tiles * size), jnp.float32),
                 pltpu.VMEM((rows, size, tiles * size), jnp.bfloat16),
+                pltpu.VMEM((rows, products, size, size), jnp.bfloat16),
                 pltpu.SemaphoreType.DMA((5,)),
+                pltpu.SemaphoreType.DMA((rows,)),
                 pltpu.SemaphoreType.REGULAR,
                 pltpu.SemaphoreType.DMA((2, 5, 2 * rows)),
                 pltpu.SemaphoreType.DMA((2, 5, 2 * rows)),

time: 45.9 us -> 45.2 us (0.985)
  Pallas kernels: 43.9 us -> 43.3 us
    pallas_call x1, Pallas kernels: 43.9 us -> 43.3 us  [per_device(): pl.pallas_call(functools.partial(kernel, doms), out_shape=jax.ShapeDtypeS...]
where the time goes in v1:
time: 45.2 us; the launch traced here: 45 us
  Pallas kernels  43.3 us (96%)
  local copies, waits for them, and re-layouts  1.77 us (4%)
    pallas_call x1, Pallas kernels, per_device(): pl.pallas_call(functools.partial(kernel, doms), out_shape=jax.ShapeDtypeS...  43.3 us
    unnamed x1, local copies, waits for them, and re-layouts  1.77 us

profile of v1, /device:TPU:1, one launch (start us, length us, event | category | flops | bytes accessed | tf_op | source)
XLA Modules:
  0.0 45.0 jit_solution(8399738099340276730)
XLA Ops:
  0.0 43.3 %shard_map.46 = bf16[3,4,128,128]{3,2,1,0:T(8,128)(2,1)} custom-call(bf16[3,12,128,128]{3,2,1,0:T(8,128)(2,1)} %p_hbm.1, s32[3,12]{1,0:T(4,128)} %cols_hbm.1, s32[3,4,12]{2,1,0:T(4,128)} %sel_square_hbm.1, s32[3,4,12]{2,1,0:T(4,128)} %sel_cube_hbm.1), custom_call_target="tpu_custom_call" | custom-call | flops 1207959552 | bytes 2359296 | tf_op jit(solution)/shard_map/pallas_call | solution.py:319
  43.3 1.8 %copy.6 = bf16[3,4,128,128]{3,2,1,0:T(8,128)(2,1)} copy(bf16[3,4,128,128]{3,2,1,0:T(8,128)(2,1)} %shard_map.46) | data formatting | bytes 786432

commit v2 on v1

--- a/solution.py
+++ b/solution.py
@@ -284,11 +284,11 @@
     q1.pass_on()
     q1.send_rest()
     q0.take_across()
+    q1.send_across()
+    q1.take_rest()
     turn(square0, rows * tiles, zero_q, sooner + later)
     for i in range(rows):
         first_out[i] = purified(0, i)
-    q1.send_across()
-    q1.take_rest()
     turn(square1, rows * tiles, zero_q, sooner)
     q1.take_across()
     turn(square1, rows * tiles, zero_q, later)

time: 45.2 us -> 45.2 us (level)
  no operation moved by 1% of the time
where the time goes in v2:
time: 45.2 us; the launch traced here: 45 us
  Pallas kernels  43.3 us (96%)
  local copies, waits for them, and re-layouts  1.77 us (4%)
    pallas_call x1, Pallas kernels, per_device(): pl.pallas_call(functools.partial(kernel, doms), out_shape=jax.ShapeDtypeS...  43.3 us
    unnamed x1, local copies, waits for them, and re-layouts  1.77 us

profile of v2, /device:TPU:1, one launch (start us, length us, event | category | flops | bytes accessed | tf_op | source)
XLA Modules:
  0.0 45.0 jit_solution(7403660339899782007)
XLA Ops:
  0.0 43.3 %shard_map.46 = bf16[3,4,128,128]{3,2,1,0:T(8,128)(2,1)} custom-call(bf16[3,12,128,128]{3,2,1,0:T(8,128)(2,1)} %p_hbm.1, s32[3,12]{1,0:T(4,128)} %cols_hbm.1, s32[3,4,12]{2,1,0:T(4,128)} %sel_square_hbm.1, s32[3,4,12]{2,1,0:T(4,128)} %sel_cube_hbm.1), custom_call_target="tpu_custom_call" | custom-call | flops 1207959552 | bytes 2359296 | tf_op jit(solution)/shard_map/pallas_call | solution.py:319
  43.3 1.8 %copy.6 = bf16[3,4,128,128]{3,2,1,0:T(8,128)(2,1)} copy(bf16[3,4,128,128]{3,2,1,0:T(8,128)(2,1)} %shard_map.46) | data formatting | bytes 786432
